TPU v7x, 32 devices: a whole 2x2x4 slice. The times are simulated.
32 devices in a mesh: grp: 2 (over y), obs: 4 (over z), par: 4 (over x, core).
Axes of the slice: x: 2, y: 2, z: 4, core: 2. Of those that a mesh axis runs over, the one named last changes fastest.
Arguments:
- predicted: bfloat16 [256, 786432], P(None, ('grp', 'obs', 'par')), parts along dimension 1, may hold values from -120 to 120
- observed: float32 [786432], P(('grp', 'obs', 'par')), parts along dimension 0, may hold values from -120 to 120
- band: float32 [8, 786432], P(None, ('grp', 'obs', 'par')), parts along dimension 1, may hold values from -5 to 5
- offsets: int32 [8], replicated, may hold values from -1024 to 1024, as said below
- rows_count: int32 [32], P(('grp', 'obs', 'par')), parts along dimension 0, may hold values from 12288 to 23552, as said below
- params: bfloat16 [16384, 256], P(('grp', 'obs', 'par')), parts along dimension 0, may hold values from -6 to 6
Outputs:
- params_new: float32 [16384, 256], P(('grp', 'obs', 'par')), parts along dimension 0
- whitened_misfit: float32 [786432], P(('grp', 'obs', 'par')), parts along dimension 0
There are 2 independent parts, one for each index of `grp`. A program takes and returns all parts, laid end to end along the dimension named above; an argument that names none is the same for every part. Nothing has to cross between parts.
Inputs may be any that keep to these rules, and one draw needn't show every extreme that they name: offsets[0] is 0, the 8 offsets are distinct, and both -1024 and 1024 are among them. `rows_count`: every shard holds this many strain observations first, then load observations up to its last 1024 observations, which are strain observations again; in every draw some shard holds exactly 23552 leading strain observations and some exactly 12288.
All inputs are finite; a program needn't handle non-finite values.
Results may differ from a plain program's by a relative error of at most 0.0029.
Values may be sent and summed in bfloat16 or wider, within the bound.
A program may use at most 256 MiB of HBM per device.

v0:
```python
import functools
import math

import jax
import jax.numpy as jnp
from jax import lax
from jax.experimental import pallas as pl
from jax.experimental.pallas import tpu as pltpu
from jax.sharding import PartitionSpec as P

H = 1024
LANES = 128
ROWS = 32
EXTRA = 16
BLOCK = 32
MESH = pl.DeviceIdType.MESH


def whiten_kernel(
    tiles, off_ref, count_ref, pred_ref, left_ref, right_ref, obs_ref, obs_left_ref, obs_right_ref, band_ref,
    acc_ref, misfit_ref, anomaly, innovation, coef, white,
):
    step = pl.program_id(0)
    members = pred_ref.shape[0]
    terms = band_ref.shape[0]

    def enter(pred, obs):
        wide = pred.astype(jnp.float32)
        mean = jnp.sum(wide, axis=0, keepdims=True) * (1.0 / members)
        at = pl.ds(pl.multiple_of(step * H, H), H)
        anomaly[:, at] = (wide - mean).astype(jnp.bfloat16)
        innov = (obs - mean).astype(jnp.bfloat16).astype(jnp.float32)
        innovation[:, at] = jnp.broadcast_to(innov, (8, H))

    @pl.when(step == 0)
    def _():
        enter(left_ref[...], obs_left_ref[...])
        acc_ref[...] = jnp.zeros_like(acc_ref)

    @pl.when((step > 0) & (step <= tiles))
    def _():
        enter(pred_ref[...], obs_ref[...])

    @pl.when(step == tiles + 1)
    def _():
        enter(right_ref[...], obs_right_ref[...])

    @pl.when(step >= 2)
    def _():
        tile = step - 2
        local = tile * H + lax.broadcasted_iota(jnp.int32, (1, H), 1)
        strain = ((local < count_ref[0]) | (local >= (tiles - 1) * H)).astype(jnp.float32)
        lane = lax.broadcasted_iota(jnp.int32, (ROWS, LANES), 1)
        lane8 = lax.broadcasted_iota(jnp.int32, (8, LANES), 1)
        starts, shifts, cuts = [], [], []
        for k in range(terms):
            begin = (tile + 1) * H + off_ref[k]
            rest = lax.rem(begin, LANES)
            starts.append(begin - rest)
            shifts.append(lax.rem(LANES - rest, LANES))
            cuts.append(LANES - rest)
        pieces = H // LANES
        row_sum = [None] * pieces
        for k in range(terms):
            factor = band_ref[k : k + 1, :]
            if k:
                factor = factor * strain
            coef[k] = jnp.broadcast_to(factor, (ROWS, H)).astype(jnp.bfloat16)
            rolled = [
                pltpu.roll(
                    innovation[:, pl.ds(pl.multiple_of(starts[k] + j * LANES, LANES), LANES)], shifts[k], 1
                )
                for j in range(pieces + 1)
            ]
            for j in range(pieces):
                part = jnp.where(lane8 < cuts[k], rolled[j], rolled[j + 1])[0:1, :]
                part = part * factor[:, j * LANES : (j + 1) * LANES]
                row_sum[j] = part if k == 0 else row_sum[j] + part
        row = jnp.concatenate(row_sum, axis=1)
        misfit_ref[...] = row
        high = row.astype(jnp.bfloat16).astype(jnp.float32)
        which = lax.broadcasted_iota(jnp.int32, (EXTRA, H), 0)
        extra = jnp.where(which == 0, high, jnp.where(which == 1, row - high, 0.0))
        white[members : members + EXTRA, :] = extra.astype(jnp.bfloat16)

        def rows(chunk, carry):
            here = pl.ds(pl.multiple_of(chunk * ROWS, ROWS), ROWS)
            sums = [None] * pieces
            for k in range(terms):
                before = None
                for j in range(pieces + 1):
                    block = anomaly[here, pl.ds(pl.multiple_of(starts[k] + j * LANES, LANES), LANES)]
                    rolled = pltpu.roll(block.astype(ROLL), shifts[k], 1)
                    if j:
                        part = jnp.where(lane < cuts[k], before, rolled).astype(ACC)
                        part = part * coef[k, :, (j - 1) * LANES : j * LANES].astype(ACC)
                        sums[j - 1] = part if k == 0 else sums[j - 1] + part
                    before = rolled
            for j in range(pieces):
                white[here, j * LANES : (j + 1) * LANES] = sums[j].astype(jnp.bfloat16)
            return carry

        lax.fori_loop(0, members // ROWS, rows, 0)
        acc_ref[...] += lax.dot_general(
            white[...], white[0:members, :], (((1,), (1,)), ((), ())), preferred_element_type=jnp.float32
        )


ROLL = jnp.bfloat16
ACC = jnp.bfloat16


def whiten_gram(offsets, count, predicted, left, right, observed, obs_left, obs_right, band):
    members, columns = predicted.shape
    terms = band.shape[0]
    tiles = columns // H
    smem = pl.BlockSpec(memory_space=pltpu.SMEM)
    enter = lambda s: (0, jnp.clip(s - 1, 0, tiles - 1))
    leave = lambda s: (0, jnp.clip(s - 2, 0, tiles - 1))
    fixed = lambda s: (0, 0)
    return pl.pallas_call(
        functools.partial(whiten_kernel, tiles),
        grid=(tiles + 2,),
        out_shape=(
            jax.ShapeDtypeStruct((members + EXTRA, members), jnp.float32),
            jax.ShapeDtypeStruct((1, columns), jnp.float32),
        ),
        in_specs=[
            smem, smem,
            pl.BlockSpec((members, H), enter),
            pl.BlockSpec((members, H), fixed),
            pl.BlockSpec((members, H), fixed),
            pl.BlockSpec((1, H), enter),
            pl.BlockSpec((1, H), fixed),
            pl.BlockSpec((1, H), fixed),
            pl.BlockSpec((terms, H), leave),
        ],
        out_specs=(
            pl.BlockSpec((members + EXTRA, members), fixed),
            pl.BlockSpec((1, H), leave),
        ),
        scratch_shapes=[
            pltpu.VMEM((members, columns + 2 * H + LANES), jnp.bfloat16),
            pltpu.VMEM((8, columns + 2 * H + LANES), jnp.float32),
            pltpu.VMEM((terms, ROWS, H), jnp.bfloat16),
            pltpu.VMEM((members + EXTRA, H), jnp.bfloat16),
        ],
        compiler_params=pltpu.CompilerParams(vmem_limit_bytes=48 << 20),
    )(offsets, count, predicted, left, right, observed, obs_left, obs_right, band)


def sum_kernel(shards, x_ref, out_ref, arrived, chunks, send_a, recv_a, send_b, recv_b):
    lines = arrived.shape[1]
    grp = lax.axis_index("grp")
    par_size = lax.axis_size("par")
    me = lax.axis_index("obs") * par_size + lax.axis_index("par")

    def where(d):
        peer = lax.rem(me + d, shards)
        return peer, (grp, peer // par_size, lax.rem(peer, par_size))

    barrier = pltpu.get_barrier_semaphore()
    for d in range(1, shards):
        pl.semaphore_signal(barrier, inc=1, device_id=where(d)[1], device_id_type=MESH)
    pl.semaphore_wait(barrier, shards - 1)
    first = []
    for d in range(1, shards):
        peer, device = where(d)
        copy = pltpu.make_async_remote_copy(
            src_ref=x_ref.at[peer], dst_ref=arrived.at[d],
            send_sem=send_a.at[d], recv_sem=recv_a.at[d], device_id=device, device_id_type=MESH,
        )
        copy.start()
        first.append(copy)
    total = x_ref[me]
    for d in range(1, shards):
        first[d - 1].wait()
        total = total + arrived[d]
    proj = total[lines - 8 : lines, :]
    chunks[...] = total[0 : lines - 8, :]
    size = lines - 8
    mine = pl.ds(pl.multiple_of(me * size, size), size)
    second = []
    for d in range(1, shards):
        peer, device = where(d)
        copy = pltpu.make_async_remote_copy(
            src_ref=chunks, dst_ref=out_ref.at[mine],
            send_sem=send_b.at[d], recv_sem=recv_b.at[d], device_id=device, device_id_type=MESH,
        )
        copy.start()
        second.append(copy)
    out_ref[mine, :] = chunks[...]
    out_ref[shards * size : shards * size + 8, :] = proj
    for d in range(1, shards):
        second[d - 1].wait()


def sum_over_shards(acc, shards):
    members = acc.shape[1]
    if shards > 1 and members % shards == 0 and (members // shards) % 8 == 0:
        size = members // shards
        chunks = acc[:members].reshape(shards, size, members)
        tail = jnp.broadcast_to(acc[members : members + 8][None], (shards, 8, members))
        vmem = pl.BlockSpec(memory_space=pltpu.VMEM)
        return pl.pallas_call(
            functools.partial(sum_kernel, shards),
            out_shape=jax.ShapeDtypeStruct((members + 8, members), jnp.float32),
            in_specs=[vmem],
            out_specs=vmem,
            scratch_shapes=[
                pltpu.VMEM((shards, size + 8, members), jnp.float32),
                pltpu.VMEM((size, members), jnp.float32),
                pltpu.SemaphoreType.DMA((shards,)),
                pltpu.SemaphoreType.DMA((shards,)),
                pltpu.SemaphoreType.DMA((shards,)),
                pltpu.SemaphoreType.DMA((shards,)),
            ],
            compiler_params=pltpu.CompilerParams(collective_id=0, has_side_effects=True),
        )(jnp.concatenate([chunks, tail], axis=1))
    return lax.psum(acc[: members + 8], ("obs", "par"))


def exact(a, b, dims):
    return lax.dot_general(
        a, b, (dims, ((), ())), precision=lax.Precision.HIGHEST, preferred_element_type=jnp.float32
    )


def transform_kernel(obs_total, x_ref, out_ref, left, right):
    members = out_ref.shape[0]
    scale = 1.0 / obs_total
    line = lax.broadcasted_iota(jnp.int32, (members, members), 0)
    column = lax.broadcasted_iota(jnp.int32, (members, members), 1)
    eye = (line == column).astype(jnp.float32)
    left[...] = x_ref[0:members, :] * scale + eye
    right[...] = eye
    small_line = lax.broadcasted_iota(jnp.int32, (BLOCK, 1), 0)
    small = (
        lax.broadcasted_iota(jnp.int32, (BLOCK, BLOCK), 0) == lax.broadcasted_iota(jnp.int32, (BLOCK, BLOCK), 1)
    ).astype(jnp.float32)
    for b in range(members // BLOCK):
        lo, hi = b * BLOCK, (b + 1) * BLOCK
        a = left[lo:hi, lo:hi]
        x = small
        for j in range(BLOCK):
            factor = a[:, j : j + 1] / a[j : j + 1, j : j + 1]
            factor = jnp.where(small_line > j, factor, 0.0)
            x = x - factor * x[j : j + 1, :]
            a = a - factor * a[j : j + 1, :]
        diagonal = jnp.sum(a * small, axis=1, keepdims=True)
        x = x * lax.rsqrt(diagonal)
        panel_left = exact(x, left[lo:hi, :], ((1,), (0,)))
        panel_right = exact(x, right[lo:hi, :], ((1,), (0,)))
        right[lo:hi, :] = panel_right
        if hi < members:
            outer = panel_left
            update_left = exact(outer, panel_left, ((0,), (0,)))
            update_right = exact(outer, panel_right, ((0,), (0,)))
            left[hi:, :] = left[hi:, :] - update_left[hi:, :]
            right[hi:, :] = right[hi:, :] - update_right[hi:, :]
    inverse = right[...]
    projection = (x_ref[members : members + 1, :] + x_ref[members + 1 : members + 2, :]) * (
        math.sqrt(members - 1) / obs_total
    )
    half = jnp.sum(inverse * projection, axis=1, keepdims=True)
    weights = exact(inverse, jnp.broadcast_to(half, (members, LANES)), ((0,), (0,)))[:, 0:1]
    out_ref[...] = inverse.T + weights * (1.0 / math.sqrt(members - 1))


def transform_of(total, obs_total):
    members = total.shape[1]
    return pl.pallas_call(
        functools.partial(transform_kernel, obs_total),
        out_shape=jax.ShapeDtypeStruct((members, members), jnp.float32),
        scratch_shapes=[pltpu.VMEM((members, members), jnp.float32)] * 2,
        compiler_params=pltpu.CompilerParams(vmem_limit_bytes=32 << 20),
    )(total)


def body(predicted, observed, band, offsets, rows_count, params):
    members = predicted.shape[0]
    columns = predicted.shape[1]
    axes = ("obs", "par")
    shards = lax.axis_size(axes)
    obs_total = columns * shards
    misfit_factor = math.sqrt((members - 1) / obs_total)
    up = [(i, i + 1) for i in range(shards - 1)]
    down = [(j, i) for i, j in up]
    obs_row = observed[None, :]
    left = lax.ppermute(predicted[:, columns - H :], axes, up)
    right = lax.ppermute(predicted[:, :H], axes, down)
    obs_left = lax.ppermute(obs_row[:, columns - H :], axes, up)
    obs_right = lax.ppermute(obs_row[:, :H], axes, down)
    acc, row = whiten_gram(
        offsets, rows_count, predicted, left, right, obs_row, obs_left, obs_right, band
    )
    total = sum_over_shards(acc, shards)
    transform = transform_of(total, obs_total)
    params_wide = params.astype(jnp.float32)
    param_mean = jnp.mean(params_wide, axis=1, keepdims=True)
    params_new = param_mean + jnp.dot(
        params_wide - param_mean, transform, precision=lax.Precision.HIGHEST
    )
    return (params_new, row[0] * misfit_factor)


def solution(mesh):
    in_specs = (
        P(None, ("grp", "obs", "par")),
        P(("grp", "obs", "par")),
        P(None, ("grp", "obs", "par")),
        P(),
        P(("grp", "obs", "par")),
        P(("grp", "obs", "par"), None),
    )
    out_specs = (P(("grp", "obs", "par"), None), P(("grp", "obs", "par")))
    return jax.shard_map(body, mesh=mesh, in_specs=in_specs, out_specs=out_specs, check_vma=False)
```

profile of v0, /device:TPU:0, one launch (start us, length us, event | category | flops | bytes accessed | tf_op | source)
XLA Modules:
  0.0 143.5 jit_solution(14345456001026504492)
XLA Ops:
  0.6 0.0 copy-start.4
  0.6 1.3 fusion.1
  2.0 2.4 %collective-permute-start = (bf16[256,1024]{1,0:T(8,128)(2,1)S(1)}, bf16[256,1024]{1,0:T(8,128)(2,1)S(1)}, u32[]{:S(2)}, u32[]{:S(2)}) collective-permute-start(bf16[256,1024]{1,0:T(8,128)(2,1)S(1)} %get-tuple-element.7), channel_id=1, source_target_pairs={{0,1},{1,2},{2,3},{3,4},{4,5},{5,6},{6,7},{7,8},{8,9},{9,10},{10,1... | collective-permute-start | bytes 1572872 | tf_op jit(solution)/shard_map/ppermute | solution.py:290
  4.4 1.3 collective-permute-start.1
  5.7 0.7 fusion.2
  6.4 5.1 %collective-permute-start.2 = (f32[1,1024]{1,0:T(1,128)S(1)}, f32[1,1024]{1,0:T(1,128)S(1)}, u32[]{:S(2)}, u32[]{:S(2)}) collective-permute-start(f32[1,1024]{1,0:T(1,128)S(1)} %get-tuple-element.9), channel_id=1, source_target_pairs={{0,1},{1,2},{2,3},{3,4},{4,5},{5,6},{6,7},{7,8},{8,9},{9,10},{10,1... | collective-permute-start | bytes 12296 | tf_op jit(solution)/shard_map/ppermute | solution.py:292
  11.5 1.3 collective-permute-start.3
  12.8 1.1 convert_reduce_fusion
  14.5 0.0 collective-permute-done.2.obs_left_ref
  14.5 1.2 collective-permute-done.3.obs_right_ref
  15.8 0.0 collective-permute-done.left_ref
  15.8 0.0 collective-permute-done.1.right_ref
  15.8 0.0 copy-start.1
  15.8 1.1 copy-done.1
  16.9 0.0 copy-start.2
  16.9 0.9 copy-done.2
  17.8 0.0 copy-start.3
  17.8 0.7 copy-done.3
  18.5 68.2 %shard_map.77 = (f32[272,256]{1,0:T(8,128)S(1)}, f32[1,24576]{1,0:T(1,128)S(1)}) custom-call(s32[8]{0:T(128)S(1)} %copy-done.3, s32[1]{0:T(128)S(6)} %copy.8.count_ref, bf16[256,24576]{1,0:T(8,128)(2,1)} %pred_ref.1, bf16[256,1024]{1,0:T(8,128)(2,1)S(1)} %collective-permute-done.left_ref, bf16[256,1024]{1,0:T(8,128)(2,1)S(1)} %collective-permute-done.1.right_ref, ...), custom_call_target="tpu_custom_call" | custom-call | tf_op jit(solution)/shard_map/pallas_call | solution.py:121
  86.8 0.8 pad_maximum_fusion.x_ref
  87.5 25.2 %shard_map.78.x_ref = f32[264,256]{1,0:T(8,128)} custom-call(f32[16,24,256]{2,1,0:T(8,128)} %pad_maximum_fusion.x_ref), custom_call_target="tpu_custom_call" | custom-call | tf_op jit(solution)/shard_map/pallas_call | solution.py:205
  112.7 0.0 copy-start
  112.7 0.9 copy-done
  113.7 27.7 %shard_map.79 = f32[256,256]{1,0:T(8,128)S(1)} custom-call(f32[264,256]{1,0:T(8,128)S(1)} %copy-done), custom_call_target="tpu_custom_call" | custom-call | tf_op jit(solution)/shard_map/pallas_call | solution.py:272
  141.3 0.7 broadcast_multiply_fusion
  142.1 0.0 copy-done.4
  142.1 1.4 convolution_add_fusion
  (4 shorter events, 0.0 us)
Async XLA Ops:
  0.6 141.4 %copy-start.4 = (bf16[512,256]{1,0:T(8,128)(2,1)S(1)}, bf16[512,256]{1,0:T(8,128)(2,1)}, u32[]{:S(2)}) copy-start(bf16[512,256]{1,0:T(8,128)(2,1)} %param.11) | copy-start | bytes 786436
  2.0 13.8 %collective-permute-start = (bf16[256,1024]{1,0:T(8,128)(2,1)S(1)}, bf16[256,1024]{1,0:T(8,128)(2,1)S(1)}, u32[]{:S(2)}, u32[]{:S(2)}) collective-permute-start(bf16[256,1024]{1,0:T(8,128)(2,1)S(1)} %get-tuple-element.7), channel_id=1, source_target_pairs={{0,1},{1,2},{2,3},{3,4},{4,5},{5,6},{6,7},{7,8},{8,9},{9,10},{10,1... | collective-permute-start | bytes 1572872 | tf_op jit(solution)/shard_map/ppermute | solution.py:290
  4.4 11.4 %collective-permute-start.1 = (bf16[256,1024]{1,0:T(8,128)(2,1)S(1)}, bf16[256,1024]{1,0:T(8,128)(2,1)S(1)}, u32[]{:S(2)}, u32[]{:S(2)}) collective-permute-start(bf16[256,1024]{1,0:T(8,128)(2,1)S(1)} %get-tuple-element.6), channel_id=1, source_target_pairs={{1,0},{2,1},{3,2},{4,3},{5,4},{6,5},{7,6},{8,7},{9,8},{10,9},{11,1... | collective-permute-start | bytes 1572872 | tf_op jit(solution)/shard_map/ppermute | solution.py:291
  6.4 8.2 %collective-permute-start.2 = (f32[1,1024]{1,0:T(1,128)S(1)}, f32[1,1024]{1,0:T(1,128)S(1)}, u32[]{:S(2)}, u32[]{:S(2)}) collective-permute-start(f32[1,1024]{1,0:T(1,128)S(1)} %get-tuple-element.9), channel_id=1, source_target_pairs={{0,1},{1,2},{2,3},{3,4},{4,5},{5,6},{6,7},{7,8},{8,9},{9,10},{10,1... | collective-permute-start | bytes 12296 | tf_op jit(solution)/shard_map/ppermute | solution.py:292
  11.5 4.3 %collective-permute-start.3 = (f32[1,1024]{1,0:T(1,128)S(1)}, f32[1,1024]{1,0:T(1,128)S(1)}, u32[]{:S(2)}, u32[]{:S(2)}) collective-permute-start(f32[1,1024]{1,0:T(1,128)S(1)} %get-tuple-element.8), channel_id=1, source_target_pairs={{1,0},{2,1},{3,2},{4,3},{5,4},{6,5},{7,6},{8,7},{9,8},{10,9},{11,1... | collective-permute-start | bytes 12296 | tf_op jit(solution)/shard_map/ppermute | solution.py:293
  15.8 1.1 copy-start.1
  16.9 0.9 copy-start.2
  17.8 0.7 copy-start.3
  112.7 1.0 copy-start
where the time goes:
time: 144 us; the launch traced here: 143 us
  Pallas kernels  121 us (84%)
  starting transfers between devices  10.1 us (7%)
  local copies, waits for them, and re-layouts  5.69 us (4%)
  other arithmetic  2.62 us (2%)
    pallas_call x1, Pallas kernels, whiten_gram(): pl.pallas_call(functools.partial(whiten_kernel, tiles), grid=(tiles + 2,)...  68.2 us
    pallas_call x1, Pallas kernels, transform_of(): pl.pallas_call(functools.partial(transform_kernel, obs_total), out_shape=...  27.7 us
    pallas_call x1, Pallas kernels, sum_over_shards(): pl.pallas_call(functools.partial(sum_kernel, shards), out_shape=jax.Shape...  25.2 us
    ppermute x1, starting transfers between devices, body(): obs_left = lax.ppermute(obs_row[:, columns - H:], axes, up)  5.09 us
    unnamed x10, local copies, waits for them, and re-layouts  3.63 us
  transfers between devices with their start and end apart: 4, of which 1 were waited for; matrix products, arithmetic and copies ran while one was open for 1% of the time, Pallas kernels for 0%

commit v1 on v0

--- a/solution.py
+++ b/solution.py
@@ -10,14 +10,14 @@
 
 H = 1024
 LANES = 128
-ROWS = 32
+ROWS = 64
 EXTRA = 16
 BLOCK = 32
 MESH = pl.DeviceIdType.MESH
 
 
 def whiten_kernel(
-    tiles, off_ref, count_ref, pred_ref, left_ref, right_ref, obs_ref, obs_left_ref, obs_right_ref, band_ref,
+    tiles, off_ref, count_ref, pred_ref, left_ref, right_ref, obs_ref, band_ref,
     acc_ref, misfit_ref, anomaly, innovation, coef, white,
 ):
     step = pl.program_id(0)
@@ -32,9 +32,13 @@
         innov = (obs - mean).astype(jnp.bfloat16).astype(jnp.float32)
         innovation[:, at] = jnp.broadcast_to(innov, (8, H))
 
+    def unpack(ref):
+        parts = ref[members : members + EXTRA, :].astype(jnp.float32)
+        return ref[0:members, :], parts[0:1, :] + (parts[1:2, :] + parts[2:3, :])
+
     @pl.when(step == 0)
     def _():
-        enter(left_ref[...], obs_left_ref[...])
+        enter(*unpack(left_ref))
         acc_ref[...] = jnp.zeros_like(acc_ref)
 
     @pl.when((step > 0) & (step <= tiles))
@@ -43,14 +47,14 @@
 
     @pl.when(step == tiles + 1)
     def _():
-        enter(right_ref[...], obs_right_ref[...])
+        enter(*unpack(right_ref))
 
     @pl.when(step >= 2)
     def _():
         tile = step - 2
         local = tile * H + lax.broadcasted_iota(jnp.int32, (1, H), 1)
         strain = ((local < count_ref[0]) | (local >= (tiles - 1) * H)).astype(jnp.float32)
-        lane = lax.broadcasted_iota(jnp.int32, (ROWS, LANES), 1)
+        lane = lax.broadcasted_iota(jnp.int32, (16, LANES), 1)
         lane8 = lax.broadcasted_iota(jnp.int32, (8, LANES), 1)
         starts, shifts, cuts = [], [], []
         for k in range(terms):
@@ -65,7 +69,7 @@
             factor = band_ref[k : k + 1, :]
             if k:
                 factor = factor * strain
-            coef[k] = jnp.broadcast_to(factor, (ROWS, H)).astype(jnp.bfloat16)
+            coef[k] = jnp.broadcast_to(factor.astype(jnp.bfloat16), (16, H))
             rolled = [
                 pltpu.roll(
                     innovation[:, pl.ds(pl.multiple_of(starts[k] + j * LANES, LANES), LANES)], shifts[k], 1
@@ -83,6 +87,8 @@
         extra = jnp.where(which == 0, high, jnp.where(which == 1, row - high, 0.0))
         white[members : members + EXTRA, :] = extra.astype(jnp.bfloat16)
 
+        keep = [lane < cut for cut in cuts]
+
         def rows(chunk, carry):
             here = pl.ds(pl.multiple_of(chunk * ROWS, ROWS), ROWS)
             sums = [None] * pieces
@@ -92,15 +98,21 @@
                     block = anomaly[here, pl.ds(pl.multiple_of(starts[k] + j * LANES, LANES), LANES)]
                     rolled = pltpu.roll(block.astype(ROLL), shifts[k], 1)
                     if j:
-                        part = jnp.where(lane < cuts[k], before, rolled).astype(ACC)
-                        part = part * coef[k, :, (j - 1) * LANES : j * LANES].astype(ACC)
+                        weight = coef[k, :, (j - 1) * LANES : j * LANES]
+                        part = jnp.concatenate(
+                            [
+                                jnp.where(keep[k], before[h : h + 16], rolled[h : h + 16]) * weight
+                                for h in range(0, ROWS, 16)
+                            ],
+                            axis=0,
+                        )
                         sums[j - 1] = part if k == 0 else sums[j - 1] + part
                     before = rolled
             for j in range(pieces):
                 white[here, j * LANES : (j + 1) * LANES] = sums[j].astype(jnp.bfloat16)
             return carry
 
-        lax.fori_loop(0, members // ROWS, rows, 0)
+        lax.fori_loop(0, members // ROWS, rows, 0, unroll=2)
         acc_ref[...] += lax.dot_general(
             white[...], white[0:members, :], (((1,), (1,)), ((), ())), preferred_element_type=jnp.float32
         )
@@ -110,7 +122,7 @@
 ACC = jnp.bfloat16
 
 
-def whiten_gram(offsets, count, predicted, left, right, observed, obs_left, obs_right, band):
+def whiten_gram(offsets, count, predicted, left, right, observed, band):
     members, columns = predicted.shape
     terms = band.shape[0]
     tiles = columns // H
@@ -128,11 +140,9 @@
         in_specs=[
             smem, smem,
             pl.BlockSpec((members, H), enter),
-            pl.BlockSpec((members, H), fixed),
-            pl.BlockSpec((members, H), fixed),
+            pl.BlockSpec((members + EXTRA, H), fixed),
+            pl.BlockSpec((members + EXTRA, H), fixed),
             pl.BlockSpec((1, H), enter),
-            pl.BlockSpec((1, H), fixed),
-            pl.BlockSpec((1, H), fixed),
             pl.BlockSpec((terms, H), leave),
         ],
         out_specs=(
@@ -142,11 +152,11 @@
         scratch_shapes=[
             pltpu.VMEM((members, columns + 2 * H + LANES), jnp.bfloat16),
             pltpu.VMEM((8, columns + 2 * H + LANES), jnp.float32),
-            pltpu.VMEM((terms, ROWS, H), jnp.bfloat16),
+            pltpu.VMEM((terms, 16, H), jnp.bfloat16),
             pltpu.VMEM((members + EXTRA, H), jnp.bfloat16),
         ],
         compiler_params=pltpu.CompilerParams(vmem_limit_bytes=48 << 20),
-    )(offsets, count, predicted, left, right, observed, obs_left, obs_right, band)
+    )(offsets, count, predicted, left, right, observed, band)
 
 
 def sum_kernel(shards, x_ref, out_ref, arrived, chunks, send_a, recv_a, send_b, recv_b):
@@ -249,15 +259,17 @@
             a = a - factor * a[j : j + 1, :]
         diagonal = jnp.sum(a * small, axis=1, keepdims=True)
         x = x * lax.rsqrt(diagonal)
-        panel_left = exact(x, left[lo:hi, :], ((1,), (0,)))
-        panel_right = exact(x, right[lo:hi, :], ((1,), (0,)))
-        right[lo:hi, :] = panel_right
+        first, later = lo // LANES * LANES, hi // LANES * LANES
+        top = -(-hi // LANES) * LANES
+        panel_left = exact(x, left[lo:hi, first:], ((1,), (0,)))
+        panel_right = exact(x, right[lo:hi, 0:top], ((1,), (0,)))
+        right[lo:hi, 0:top] = panel_right
         if hi < members:
-            outer = panel_left
-            update_left = exact(outer, panel_left, ((0,), (0,)))
+            outer = panel_left[:, later - first :]
+            update_left = exact(outer, outer, ((0,), (0,)))
             update_right = exact(outer, panel_right, ((0,), (0,)))
-            left[hi:, :] = left[hi:, :] - update_left[hi:, :]
-            right[hi:, :] = right[hi:, :] - update_right[hi:, :]
+            left[hi:, later:] = left[hi:, later:] - update_left[hi - later :, :]
+            right[hi:, 0:top] = right[hi:, 0:top] - update_right[hi - later :, :]
     inverse = right[...]
     projection = (x_ref[members : members + 1, :] + x_ref[members + 1 : members + 2, :]) * (
         math.sqrt(members - 1) / obs_total
@@ -275,6 +287,14 @@
         scratch_shapes=[pltpu.VMEM((members, members), jnp.float32)] * 2,
         compiler_params=pltpu.CompilerParams(vmem_limit_bytes=32 << 20),
     )(total)
+
+
+def packed_edge(pred, obs):
+    high = lax.reduce_precision(obs, 8, 7)
+    middle = lax.reduce_precision(obs - high, 8, 7)
+    low = obs - high - middle
+    parts = jnp.concatenate([high, middle, low, jnp.zeros((EXTRA - 3, H), jnp.float32)], axis=0)
+    return jnp.concatenate([pred, parts.astype(jnp.bfloat16)], axis=0)
 
 
 def body(predicted, observed, band, offsets, rows_count, params):
@@ -287,12 +307,10 @@
     up = [(i, i + 1) for i in range(shards - 1)]
     down = [(j, i) for i, j in up]
     obs_row = observed[None, :]
-    left = lax.ppermute(predicted[:, columns - H :], axes, up)
-    right = lax.ppermute(predicted[:, :H], axes, down)
-    obs_left = lax.ppermute(obs_row[:, columns - H :], axes, up)
-    obs_right = lax.ppermute(obs_row[:, :H], axes, down)
+    left = lax.ppermute(packed_edge(predicted[:, columns - H :], obs_row[:, columns - H :]), axes, up)
+    right = lax.ppermute(packed_edge(predicted[:, :H], obs_row[:, :H]), axes, down)
     acc, row = whiten_gram(
-        offsets, rows_count, predicted, left, right, obs_row, obs_left, obs_right, band
+        offsets, rows_count, predicted, left, right, obs_row, band
     )
     total = sum_over_shards(acc, shards)
     transform = transform_of(total, obs_total)

time: 144 us -> 134 us (0.931)
  starting transfers between devices: 10.1 us -> 3.68 us
  Pallas kernels: 121 us -> 115 us
  waiting for transfers between devices: 1.24 us -> 2.86 us
    pallas_call x1, Pallas kernels: 68.2 us -> 57.7 us  [whiten_gram(): pl.pallas_call(functools.partial(whiten_kernel, tiles), grid=(tiles + 2,)...]
    ppermute x4 -> x2, starting transfers between devices: 10.1 us -> 3.68 us  [the longest x1 2.39 us: body(): lax.ppermute(packed_edge(predicted[:, columns - H:], obs_row[:, columns -...]
    pallas_call x1, Pallas kernels: 25.2 us -> 30.9 us  [sum_over_shards(): pl.pallas_call(functools.partial(sum_kernel, shards), out_shape=jax.Shape...]
    ppermute x4 -> x2, waiting for transfers between devices: 1.24 us -> 2.86 us  [the longest x1 2.85 us: body(): lax.ppermute(packed_edge(predicted[:, :H], obs_row[:, :H]), axes, down)]
    pallas_call x1, Pallas kernels: 27.7 us -> 26.1 us  [transform_of(): pl.pallas_call(functools.partial(transform_kernel, obs_total), out_shape=...]
  transfers between devices with their start and end apart: 4 -> 2, of which waited for: 1 -> 1; matrix products, arithmetic and copies ran while one was open for 1% -> 1% of each run, Pallas kernels for 0% -> 0%
where the time goes in v1:
time: 134 us; the launch traced here: 133 us
  Pallas kernels  115 us (86%)
  local copies, waits for them, and re-layouts  5.62 us (4%)
  starting transfers between devices  3.68 us (3%)
  other arithmetic  3.39 us (3%)
  waiting for transfers between devices  2.86 us (2%)
  matrix products  1.42 us (1%)
  between operations  1.41 us (1%)
    pallas_call x1, Pallas kernels, whiten_gram(): pl.pallas_call(functools.partial(whiten_kernel, tiles), grid=(tiles + 2,)...  57.7 us
    pallas_call x1, Pallas kernels, sum_over_shards(): pl.pallas_call(functools.partial(sum_kernel, shards), out_shape=jax.Shape...  30.9 us
    pallas_call x1, Pallas kernels, transform_of(): pl.pallas_call(functools.partial(transform_kernel, obs_total), out_shape=...  26.1 us
    unnamed x10, local copies, waits for them, and re-layouts  3.63 us
    ppermute x1, waiting for transfers between devices, body(): lax.ppermute(packed_edge(predicted[:, :H], obs_row[:, :H]), axes, down)  2.85 us
  transfers between devices with their start and end apart: 2, of which 1 were waited for; matrix products, arithmetic and copies ran while one was open for 1% of the time, Pallas kernels for 0%

profile of v1, /device:TPU:0, one launch (start us, length us, event | category | flops | bytes accessed | tf_op | source)
XLA Modules:
  0.0 133.1 jit_solution(14628730392077662861)
XLA Ops:
  0.6 0.0 copy-start.4
  0.6 0.8 fusion.2
  1.4 1.3 fusion.3
  2.7 0.3 concatenate.15
  3.0 2.4 %collective-permute-start = (bf16[272,1024]{1,0:T(8,128)(2,1)S(1)}, bf16[272,1024]{1,0:T(8,128)(2,1)S(1)}, u32[]{:S(2)}, u32[]{:S(2)}) collective-permute-start(bf16[272,1024]{1,0:T(8,128)(2,1)S(1)} %concatenate.15), channel_id=1, source_target_pairs={{0,1},{1,2},{2,3},{3,4},{4,5},{5,6},{6,7},{7,8},{8,9},{9,10},{10,1... | collective-permute-start | bytes 1671176 | tf_op jit(solution)/shard_map/ppermute | solution.py:310
  5.4 0.3 concatenate.16
  5.8 1.3 collective-permute-start.1
  7.7 1.1 convert_reduce_fusion
  8.9 0.0 collective-permute-done.left_ref
  8.9 2.9 %collective-permute-done.1.right_ref = bf16[272,1024]{1,0:T(8,128)(2,1)S(1)} collective-permute-done((bf16[272,1024]{1,0:T(8,128)(2,1)S(1)}, bf16[272,1024]{1,0:T(8,128)(2,1)S(1)}, u32[]{:S(2)}, u32[]{:S(2)}) %collective-permute-start.1) | collective-permute-done | bytes 557088 | tf_op jit(solution)/shard_map/ppermute | solution.py:311
  11.7 0.0 copy-start.1
  11.7 1.1 copy-done.1
  12.9 0.0 copy-start.2
  12.9 0.9 copy-done.2
  13.7 0.0 copy-start.3
  13.7 0.7 copy-done.3
  14.4 57.7 %shard_map.77 = (f32[272,256]{1,0:T(8,128)S(1)}, f32[1,24576]{1,0:T(1,128)S(1)}) custom-call(s32[8]{0:T(128)S(1)} %copy-done.3, s32[1]{0:T(128)S(6)} %copy.8.count_ref, bf16[256,24576]{1,0:T(8,128)(2,1)} %pred_ref.1, bf16[272,1024]{1,0:T(8,128)(2,1)S(1)} %collective-permute-done.left_ref, bf16[272,1024]{1,0:T(8,128)(2,1)S(1)} %collective-permute-done.1.right_ref, ...), custom_call_target="tpu_custom_call" | custom-call | tf_op jit(solution)/shard_map/pallas_call | solution.py:133
  72.2 0.7 broadcast_multiply_fusion
  72.9 0.8 pad_maximum_fusion.x_ref
  73.7 30.9 %shard_map.78.x_ref = f32[264,256]{1,0:T(8,128)} custom-call(f32[16,24,256]{2,1,0:T(8,128)} %pad_maximum_fusion.x_ref), custom_call_target="tpu_custom_call" | custom-call | tf_op jit(solution)/shard_map/pallas_call | solution.py:215
  104.6 0.0 copy-start
  104.6 0.9 copy-done
  105.6 26.1 %shard_map.79 = f32[256,256]{1,0:T(8,128)S(1)} custom-call(f32[264,256]{1,0:T(8,128)S(1)} %copy-done), custom_call_target="tpu_custom_call" | custom-call | tf_op jit(solution)/shard_map/pallas_call | solution.py:284
  131.7 0.0 copy-done.4
  131.7 1.4 %convolution_add_fusion = f32[512,256]{1,0:T(8,128)} fusion(f32[256,256]{1,0:T(8,128)S(1)} %shard_map.79, bf16[512,256]{1,0:T(8,128)(2,1)S(1)} %copy-done.4, f32[512]{0:T(512)S(1)} %broadcast_multiply_fusion.1), kind=kOutput, calls=%fused_computation | convolution fusion | flops 403046400 | bytes 1050624 | tf_op jit(solution)/shard_map/dot_general | solution.py:319
  (5 shorter events, 0.0 us)
Async XLA Ops:
  0.6 131.1 %copy-start.4 = (bf16[512,256]{1,0:T(8,128)(2,1)S(1)}, bf16[512,256]{1,0:T(8,128)(2,1)}, u32[]{:S(2)}) copy-start(bf16[512,256]{1,0:T(8,128)(2,1)} %param.11) | copy-start | bytes 786436
  3.0 5.8 %collective-permute-start = (bf16[272,1024]{1,0:T(8,128)(2,1)S(1)}, bf16[272,1024]{1,0:T(8,128)(2,1)S(1)}, u32[]{:S(2)}, u32[]{:S(2)}) collective-permute-start(bf16[272,1024]{1,0:T(8,128)(2,1)S(1)} %concatenate.15), channel_id=1, source_target_pairs={{0,1},{1,2},{2,3},{3,4},{4,5},{5,6},{6,7},{7,8},{8,9},{9,10},{10,1... | collective-permute-start | bytes 1671176 | tf_op jit(solution)/shard_map/ppermute | solution.py:310
  5.8 5.9 %collective-permute-start.1 = (bf16[272,1024]{1,0:T(8,128)(2,1)S(1)}, bf16[272,1024]{1,0:T(8,128)(2,1)S(1)}, u32[]{:S(2)}, u32[]{:S(2)}) collective-permute-start(bf16[272,1024]{1,0:T(8,128)(2,1)S(1)} %concatenate.16), channel_id=1, source_target_pairs={{1,0},{2,1},{3,2},{4,3},{5,4},{6,5},{7,6},{8,7},{9,8},{10,9},{11,1... | collective-permute-start | bytes 1671176 | tf_op jit(solution)/shard_map/ppermute | solution.py:311
  11.7 1.1 copy-start.1
  12.9 0.9 copy-start.2
  13.7 0.7 copy-start.3
  104.6 1.0 copy-start

commit v2 on v1

--- a/solution.py
+++ b/solution.py
@@ -112,7 +112,7 @@
                 white[here, j * LANES : (j + 1) * LANES] = sums[j].astype(jnp.bfloat16)
             return carry
 
-        lax.fori_loop(0, members // ROWS, rows, 0, unroll=2)
+        lax.fori_loop(0, members // ROWS, rows, 0, unroll=4)
         acc_ref[...] += lax.dot_general(
             white[...], white[0:members, :], (((1,), (1,)), ((), ())), preferred_element_type=jnp.float32
         )

time: 134 us -> 129 us (0.963)
  Pallas kernels: 115 us -> 110 us
    pallas_call x1, Pallas kernels: 57.7 us -> 53.3 us  [whiten_gram(): pl.pallas_call(functools.partial(whiten_kernel, tiles), grid=(tiles + 2,)...]
where the time goes in v2:
time: 129 us
  Pallas kernels  110 us (85%)
  local copies, waits for them, and re-layouts  5.62 us (4%)
  starting transfers between devices  3.68 us (3%)
  other arithmetic  3.39 us (3%)
  waiting for transfers between devices  2.86 us (2%)
  matrix products  1.42 us (1%)
  between operations  1.41 us (1%)
    pallas_call x1, Pallas kernels, whiten_gram(): pl.pallas_call(functools.partial(whiten_kernel, tiles), grid=(tiles + 2,)...  53.3 us
    pallas_call x1, Pallas kernels, sum_over_shards(): pl.pallas_call(functools.partial(sum_kernel, shards), out_shape=jax.Shape...  30.9 us
    pallas_call x1, Pallas kernels, transform_of(): pl.pallas_call(functools.partial(transform_kernel, obs_total), out_shape=...  26.1 us
    unnamed x10, local copies, waits for them, and re-layouts  3.63 us
    ppermute x1, waiting for transfers between devices, body(): lax.ppermute(packed_edge(predicted[:, :H], obs_row[:, :H]), axes, down)  2.85 us
  transfers between devices with their start and end apart: 2, of which 1 were waited for; matrix products, arithmetic and copies ran while one was open for 1% of the time, Pallas kernels for 0%

profile of v2, /device:TPU:0, one launch (start us, length us, event | category | flops | bytes accessed | tf_op | source)
XLA Modules:
  0.0 128.7 jit_solution(8623951316470690555)
XLA Ops:
  0.6 0.0 copy-start.4
  0.6 0.8 fusion.2
  1.4 1.3 fusion.3
  2.7 0.3 concatenate.15
  3.0 2.4 %collective-permute-start = (bf16[272,1024]{1,0:T(8,128)(2,1)S(1)}, bf16[272,1024]{1,0:T(8,128)(2,1)S(1)}, u32[]{:S(2)}, u32[]{:S(2)}) collective-permute-start(bf16[272,1024]{1,0:T(8,128)(2,1)S(1)} %concatenate.15), channel_id=1, source_target_pairs={{0,1},{1,2},{2,3},{3,4},{4,5},{5,6},{6,7},{7,8},{8,9},{9,10},{10,1... | collective-permute-start | bytes 1671176 | tf_op jit(solution)/shard_map/ppermute | solution.py:310
  5.4 0.3 concatenate.16
  5.8 1.3 %collective-permute-start.1 = (bf16[272,1024]{1,0:T(8,128)(2,1)S(1)}, bf16[272,1024]{1,0:T(8,128)(2,1)S(1)}, u32[]{:S(2)}, u32[]{:S(2)}) collective-permute-start(bf16[272,1024]{1,0:T(8,128)(2,1)S(1)} %concatenate.16), channel_id=1, source_target_pairs={{1,0},{2,1},{3,2},{4,3},{5,4},{6,5},{7,6},{8,7},{9,8},{10,9},{11,1... | collective-permute-start | bytes 1671176 | tf_op jit(solution)/shard_map/ppermute | solution.py:311
  7.7 1.1 convert_reduce_fusion
  8.9 0.0 collective-permute-done.left_ref
  8.9 2.9 %collective-permute-done.1.right_ref = bf16[272,1024]{1,0:T(8,128)(2,1)S(1)} collective-permute-done((bf16[272,1024]{1,0:T(8,128)(2,1)S(1)}, bf16[272,1024]{1,0:T(8,128)(2,1)S(1)}, u32[]{:S(2)}, u32[]{:S(2)}) %collective-permute-start.1) | collective-permute-done | bytes 557088 | tf_op jit(solution)/shard_map/ppermute | solution.py:311
  11.7 0.0 copy-start.1
  11.7 1.1 copy-done.1
  12.9 0.0 copy-start.2
  12.9 0.9 copy-done.2
  13.7 0.0 copy-start.3
  13.7 0.7 copy-done.3
  14.4 53.3 %shard_map.77 = (f32[272,256]{1,0:T(8,128)S(1)}, f32[1,24576]{1,0:T(1,128)S(1)}) custom-call(s32[8]{0:T(128)S(1)} %copy-done.3, s32[1]{0:T(128)S(6)} %copy.8.count_ref, bf16[256,24576]{1,0:T(8,128)(2,1)} %pred_ref.1, bf16[272,1024]{1,0:T(8,128)(2,1)S(1)} %collective-permute-done.left_ref, bf16[272,1024]{1,0:T(8,128)(2,1)S(1)} %collective-permute-done.1.right_ref, ...), custom_call_target="tpu_custom_call" | custom-call | tf_op jit(solution)/shard_map/pallas_call | solution.py:133
  67.7 0.7 broadcast_multiply_fusion
  68.5 0.8 pad_maximum_fusion.x_ref
  69.3 30.9 %shard_map.78.x_ref = f32[264,256]{1,0:T(8,128)} custom-call(f32[16,24,256]{2,1,0:T(8,128)} %pad_maximum_fusion.x_ref), custom_call_target="tpu_custom_call" | custom-call | tf_op jit(solution)/shard_map/pallas_call | solution.py:215
  100.2 0.0 copy-start
  100.2 0.9 copy-done
  101.1 26.1 %shard_map.79 = f32[256,256]{1,0:T(8,128)S(1)} custom-call(f32[264,256]{1,0:T(8,128)S(1)} %copy-done), custom_call_target="tpu_custom_call" | custom-call | tf_op jit(solution)/shard_map/pallas_call | solution.py:284
  127.3 0.0 copy-done.4
  127.3 1.4 %convolution_add_fusion = f32[512,256]{1,0:T(8,128)} fusion(f32[256,256]{1,0:T(8,128)S(1)} %shard_map.79, bf16[512,256]{1,0:T(8,128)(2,1)S(1)} %copy-done.4, f32[512]{0:T(512)S(1)} %broadcast_multiply_fusion.1), kind=kOutput, calls=%fused_computation | convolution fusion | flops 403046400 | bytes 1050624 | tf_op jit(solution)/shard_map/dot_general | solution.py:319
  (5 shorter events, 0.0 us)
Async XLA Ops:
  0.6 126.6 %copy-start.4 = (bf16[512,256]{1,0:T(8,128)(2,1)S(1)}, bf16[512,256]{1,0:T(8,128)(2,1)}, u32[]{:S(2)}) copy-start(bf16[512,256]{1,0:T(8,128)(2,1)} %param.11) | copy-start | bytes 786436
  3.0 5.8 %collective-permute-start = (bf16[272,1024]{1,0:T(8,128)(2,1)S(1)}, bf16[272,1024]{1,0:T(8,128)(2,1)S(1)}, u32[]{:S(2)}, u32[]{:S(2)}) collective-permute-start(bf16[272,1024]{1,0:T(8,128)(2,1)S(1)} %concatenate.15), channel_id=1, source_target_pairs={{0,1},{1,2},{2,3},{3,4},{4,5},{5,6},{6,7},{7,8},{8,9},{9,10},{10,1... | collective-permute-start | bytes 1671176 | tf_op jit(solution)/shard_map/ppermute | solution.py:310
  5.8 5.9 %collective-permute-start.1 = (bf16[272,1024]{1,0:T(8,128)(2,1)S(1)}, bf16[272,1024]{1,0:T(8,128)(2,1)S(1)}, u32[]{:S(2)}, u32[]{:S(2)}) collective-permute-start(bf16[272,1024]{1,0:T(8,128)(2,1)S(1)} %concatenate.16), channel_id=1, source_target_pairs={{1,0},{2,1},{3,2},{4,3},{5,4},{6,5},{7,6},{8,7},{9,8},{10,9},{11,1... | collective-permute-start | bytes 1671176 | tf_op jit(solution)/shard_map/ppermute | solution.py:311
  11.7 1.1 copy-start.1
  12.9 0.9 copy-start.2
  13.7 0.7 copy-start.3
  100.2 1.0 copy-start

commit v3 on v2

--- a/solution.py
+++ b/solution.py
@@ -155,7 +155,7 @@
             pltpu.VMEM((terms, 16, H), jnp.bfloat16),
             pltpu.VMEM((members + EXTRA, H), jnp.bfloat16),
         ],
-        compiler_params=pltpu.CompilerParams(vmem_limit_bytes=48 << 20),
+        compiler_params=pltpu.CompilerParams(vmem_limit_bytes=62 << 20),
     )(offsets, count, predicted, left, right, observed, band)
 
 

time: 129 us -> 132 us (1.023)
  Pallas kernels: 110 us -> 113 us
    pallas_call x1, Pallas kernels: 53.3 us -> 55.3 us  [whiten_gram(): pl.pallas_call(functools.partial(whiten_kernel, tiles), grid=(tiles + 2,)...]
    unnamed x10 -> x8, local copies, waits for them, and re-layouts: 3.63 us -> 1.76 us
where the time goes in v3:
time: 132 us
  Pallas kernels  113 us (86%)
  local copies, waits for them, and re-layouts  5.38 us (4%)
  other arithmetic  4.29 us (3%)
  starting transfers between devices  3.68 us (3%)
  waiting for transfers between devices  2.85 us (2%)
  matrix products  1.42 us (1%)
  between operations  1.4 us (1%)
    pallas_call x1, Pallas kernels, whiten_gram(): pl.pallas_call(functools.partial(whiten_kernel, tiles), grid=(tiles + 2,)...  55.3 us
    pallas_call x1, Pallas kernels, sum_over_shards(): pl.pallas_call(functools.partial(sum_kernel, shards), out_shape=jax.Shape...  31.1 us
    pallas_call x1, Pallas kernels, transform_of(): pl.pallas_call(functools.partial(transform_kernel, obs_total), out_shape=...  26.1 us
    ppermute x1, waiting for transfers between devices, body(): lax.ppermute(packed_edge(predicted[:, :H], obs_row[:, :H]), axes, down)  2.84 us
  transfers between devices with their start and end apart: 2, of which 1 were waited for; matrix products, arithmetic and copies ran while one was open for 1% of the time, Pallas kernels for 0%

profile of v3, /device:TPU:0, one launch (start us, length us, event | category | flops | bytes accessed | tf_op | source)
XLA Modules:
  0.0 131.6 jit_solution(10263692722418200267)
XLA Ops:
  0.6 0.0 copy-start.1
  0.6 0.8 fusion.2
  1.4 1.3 fusion.3
  2.7 0.3 concatenate.15
  3.0 2.4 %collective-permute-start = (bf16[272,1024]{1,0:T(8,128)(2,1)S(1)}, bf16[272,1024]{1,0:T(8,128)(2,1)S(1)}, u32[]{:S(2)}, u32[]{:S(2)}) collective-permute-start(bf16[272,1024]{1,0:T(8,128)(2,1)S(1)} %concatenate.15), channel_id=1, source_target_pairs={{0,1},{1,2},{2,3},{3,4},{4,5},{5,6},{6,7},{7,8},{8,9},{9,10},{10,1... | collective-permute-start | bytes 1671176 | tf_op jit(solution)/shard_map/ppermute | solution.py:310
  5.4 0.3 concatenate.16
  5.8 1.3 collective-permute-start.1
  7.7 1.1 convert_reduce_fusion
  8.9 0.0 collective-permute-done.left_ref
  8.9 0.0 copy-start.2
  8.9 2.8 %collective-permute-done.1.right_ref = bf16[272,1024]{1,0:T(8,128)(2,1)S(1)} collective-permute-done((bf16[272,1024]{1,0:T(8,128)(2,1)S(1)}, bf16[272,1024]{1,0:T(8,128)(2,1)S(1)}, u32[]{:S(2)}, u32[]{:S(2)}) %collective-permute-start.1) | collective-permute-done | bytes 557088 | tf_op jit(solution)/shard_map/ppermute | solution.py:311
  11.7 0.0 copy-done.2
  11.7 0.0 copy-start.3
  11.7 0.8 copy-done.3
  12.5 55.3 %shard_map.77 = (f32[272,256]{1,0:T(8,128)}, f32[1,24576]{1,0:T(1,128)}) custom-call(s32[8]{0:T(128)} %off_ref.1, s32[1]{0:T(128)S(6)} %copy.8.count_ref, bf16[256,24576]{1,0:T(8,128)(2,1)} %pred_ref.1, bf16[272,1024]{1,0:T(8,128)(2,1)} %copy-done.2, bf16[272,1024]{1,0:T(8,128)(2,1)} %copy-done.3, f32[1,24576]{1,0:T(1,128)} %bitcast.6, f32[8,24576]{1,0:T(8,128)} %band_ref.1), custom_call_target="tpu_custom_call" | custom-call | tf_op jit(solution)/shard_map/pallas_call | solution.py:133
  67.9 0.7 slice.23
  68.6 1.0 slice.22
  69.5 1.6 %broadcast_multiply_fusion = f32[1,24576]{1,0:T(1,128)} fusion(f32[1,24576]{1,0:T(1,128)} %get-tuple-element.5), kind=kLoop, calls=%fused_computation.5 | loop fusion | flops 24576 | bytes 196608 | tf_op jit(solution)/shard_map/mul | solution.py:322
  71.2 0.8 pad_maximum_fusion.x_ref
  72.0 31.1 %shard_map.78.x_ref = f32[264,256]{1,0:T(8,128)} custom-call(f32[16,24,256]{2,1,0:T(8,128)} %pad_maximum_fusion.x_ref), custom_call_target="tpu_custom_call" | custom-call | tf_op jit(solution)/shard_map/pallas_call | solution.py:215
  103.1 0.0 copy-start
  103.1 0.9 copy-done
  104.1 26.1 %shard_map.79 = f32[256,256]{1,0:T(8,128)S(1)} custom-call(f32[264,256]{1,0:T(8,128)S(1)} %copy-done), custom_call_target="tpu_custom_call" | custom-call | tf_op jit(solution)/shard_map/pallas_call | solution.py:284
  130.2 0.0 copy-done.1
  130.2 1.4 %convolution_add_fusion = f32[512,256]{1,0:T(8,128)} fusion(f32[256,256]{1,0:T(8,128)S(1)} %shard_map.79, bf16[512,256]{1,0:T(8,128)(2,1)S(1)} %copy-done.1, f32[512]{0:T(512)S(1)} %broadcast_multiply_fusion.1), kind=kOutput, calls=%fused_computation | convolution fusion | flops 403046400 | bytes 1050624 | tf_op jit(solution)/shard_map/dot_general | solution.py:319
  (3 shorter events, 0.0 us)
Async XLA Ops:
  0.6 129.6 %copy-start.1 = (bf16[512,256]{1,0:T(8,128)(2,1)S(1)}, bf16[512,256]{1,0:T(8,128)(2,1)}, u32[]{:S(2)}) copy-start(bf16[512,256]{1,0:T(8,128)(2,1)} %param.11) | copy-start | bytes 786436
  3.0 5.8 %collective-permute-start = (bf16[272,1024]{1,0:T(8,128)(2,1)S(1)}, bf16[272,1024]{1,0:T(8,128)(2,1)S(1)}, u32[]{:S(2)}, u32[]{:S(2)}) collective-permute-start(bf16[272,1024]{1,0:T(8,128)(2,1)S(1)} %concatenate.15), channel_id=1, source_target_pairs={{0,1},{1,2},{2,3},{3,4},{4,5},{5,6},{6,7},{7,8},{8,9},{9,10},{10,1... | collective-permute-start | bytes 1671176 | tf_op jit(solution)/shard_map/ppermute | solution.py:310
  5.8 5.9 %collective-permute-start.1 = (bf16[272,1024]{1,0:T(8,128)(2,1)S(1)}, bf16[272,1024]{1,0:T(8,128)(2,1)S(1)}, u32[]{:S(2)}, u32[]{:S(2)}) collective-permute-start(bf16[272,1024]{1,0:T(8,128)(2,1)S(1)} %concatenate.16), channel_id=1, source_target_pairs={{1,0},{2,1},{3,2},{4,3},{5,4},{6,5},{7,6},{8,7},{9,8},{10,9},{11,1... | collective-permute-start | bytes 1671176 | tf_op jit(solution)/shard_map/ppermute | solution.py:311
  8.9 2.9 %copy-start.2 = (bf16[272,1024]{1,0:T(8,128)(2,1)}, bf16[272,1024]{1,0:T(8,128)(2,1)S(1)}, u32[]{:S(2)}) copy-start(bf16[272,1024]{1,0:T(8,128)(2,1)S(1)} %collective-permute-done.left_ref) | copy-start | bytes 1671172
  11.7 0.8 copy-start.3
  103.1 1.0 copy-start

commit v4 on v2

--- a/solution.py
+++ b/solution.py
@@ -160,7 +160,6 @@
 
 
 def sum_kernel(shards, x_ref, out_ref, arrived, chunks, send_a, recv_a, send_b, recv_b):
-    lines = arrived.shape[1]
     grp = lax.axis_index("grp")
     par_size = lax.axis_size("par")
     me = lax.axis_index("obs") * par_size + lax.axis_index("par")
@@ -186,48 +185,49 @@
     for d in range(1, shards):
         first[d - 1].wait()
         total = total + arrived[d]
-    proj = total[lines - 8 : lines, :]
-    chunks[...] = total[0 : lines - 8, :]
-    size = lines - 8
-    mine = pl.ds(pl.multiple_of(me * size, size), size)
+    chunks[...] = total
     second = []
     for d in range(1, shards):
         peer, device = where(d)
         copy = pltpu.make_async_remote_copy(
-            src_ref=chunks, dst_ref=out_ref.at[mine],
+            src_ref=chunks, dst_ref=out_ref.at[me],
             send_sem=send_b.at[d], recv_sem=recv_b.at[d], device_id=device, device_id_type=MESH,
         )
         copy.start()
         second.append(copy)
-    out_ref[mine, :] = chunks[...]
-    out_ref[shards * size : shards * size + 8, :] = proj
+    out_ref[me] = total
     for d in range(1, shards):
         second[d - 1].wait()
 
 
 def sum_over_shards(acc, shards):
     members = acc.shape[1]
-    if shards > 1 and members % shards == 0 and (members // shards) % 8 == 0:
-        size = members // shards
-        chunks = acc[:members].reshape(shards, size, members)
-        tail = jnp.broadcast_to(acc[members : members + 8][None], (shards, 8, members))
-        vmem = pl.BlockSpec(memory_space=pltpu.VMEM)
-        return pl.pallas_call(
-            functools.partial(sum_kernel, shards),
-            out_shape=jax.ShapeDtypeStruct((members + 8, members), jnp.float32),
-            in_specs=[vmem],
-            out_specs=vmem,
-            scratch_shapes=[
-                pltpu.VMEM((shards, size + 8, members), jnp.float32),
-                pltpu.VMEM((size, members), jnp.float32),
-                pltpu.SemaphoreType.DMA((shards,)),
-                pltpu.SemaphoreType.DMA((shards,)),
-                pltpu.SemaphoreType.DMA((shards,)),
-                pltpu.SemaphoreType.DMA((shards,)),
-            ],
-            compiler_params=pltpu.CompilerParams(collective_id=0, has_side_effects=True),
-        )(jnp.concatenate([chunks, tail], axis=1))
-    return lax.psum(acc[: members + 8], ("obs", "par"))
+    half = members // 2
+    direct = shards > 1 and 3 * half % (8 * shards) == 0
+    parts = shards if direct else 2
+    size = 3 * half // parts
+    gram = jnp.concatenate([acc[:members, :half], acc[half:members, half:]], axis=0).reshape(parts, size, half)
+    proj = (acc[members] + acc[members + 1]).reshape(2, 1, half)
+    tail = jnp.concatenate([proj, jnp.zeros((parts - 2, 1, half), jnp.float32)], axis=0) if parts > 2 else proj
+    packed = jnp.concatenate([gram, tail], axis=1)
+    if not direct:
+        return lax.psum(packed, ("obs", "par"))
+    vmem = pl.BlockSpec(memory_space=pltpu.VMEM)
+    return pl.pallas_call(
+        functools.partial(sum_kernel, shards),
+        out_shape=jax.ShapeDtypeStruct(packed.shape, jnp.float32),
+        in_specs=[vmem],
+        out_specs=vmem,
+        scratch_shapes=[
+            pltpu.VMEM(packed.shape, jnp.float32),
+            pltpu.VMEM(packed.shape[1:], jnp.float32),
+            pltpu.SemaphoreType.DMA((shards,)),
+            pltpu.SemaphoreType.DMA((shards,)),
+            pltpu.SemaphoreType.DMA((shards,)),
+            pltpu.SemaphoreType.DMA((shards,)),
+        ],
+        compiler_params=pltpu.CompilerParams(collective_id=0, has_side_effects=True),
+    )(packed)
 
 
 def exact(a, b, dims):
@@ -242,7 +242,18 @@
     line = lax.broadcasted_iota(jnp.int32, (members, members), 0)
     column = lax.broadcasted_iota(jnp.int32, (members, members), 1)
     eye = (line == column).astype(jnp.float32)
-    left[...] = x_ref[0:members, :] * scale + eye
+    half = members // 2
+    parts = x_ref.shape[0]
+    size = x_ref.shape[1] - 1
+    stacked = jnp.concatenate([x_ref[d, 0:size, :] for d in range(parts)], axis=0)
+    gram = jnp.concatenate(
+        [
+            jnp.concatenate([stacked[0:half], stacked[half:members].T], axis=1),
+            jnp.concatenate([stacked[half:members], stacked[members:]], axis=1),
+        ],
+        axis=0,
+    )
+    left[...] = gram * scale + eye
     right[...] = eye
     small_line = lax.broadcasted_iota(jnp.int32, (BLOCK, 1), 0)
     small = (
@@ -271,7 +282,7 @@
             left[hi:, later:] = left[hi:, later:] - update_left[hi - later :, :]
             right[hi:, 0:top] = right[hi:, 0:top] - update_right[hi - later :, :]
     inverse = right[...]
-    projection = (x_ref[members : members + 1, :] + x_ref[members + 1 : members + 2, :]) * (
+    projection = jnp.concatenate([x_ref[0, size : size + 1, :], x_ref[1, size : size + 1, :]], axis=1) * (
         math.sqrt(members - 1) / obs_total
     )
     half = jnp.sum(inverse * projection, axis=1, keepdims=True)
@@ -280,7 +291,7 @@
 
 
 def transform_of(total, obs_total):
-    members = total.shape[1]
+    members = 2 * total.shape[2]
     return pl.pallas_call(
         functools.partial(transform_kernel, obs_total),
         out_shape=jax.ShapeDtypeStruct((members, members), jnp.float32),

time: 129 us -> 125 us (0.969)
  Pallas kernels: 110 us -> 106 us
    pallas_call x1, Pallas kernels: 30.9 us -> 26.6 us  [sum_over_shards(): pl.pallas_call(functools.partial(sum_kernel, shards), out_shape=jax.Shape...]
where the time goes in v4:
time: 125 us; the launch traced here: 124 us
  Pallas kernels  106 us (85%)
  local copies, waits for them, and re-layouts  5.6 us (4%)
  starting transfers between devices  3.68 us (3%)
  other arithmetic  3.36 us (3%)
  waiting for transfers between devices  2.86 us (2%)
  matrix products  1.42 us (1%)
  between operations  1.42 us (1%)
    pallas_call x1, Pallas kernels, whiten_gram(): pl.pallas_call(functools.partial(whiten_kernel, tiles), grid=(tiles + 2,)...  53.3 us
    pallas_call x1, Pallas kernels, sum_over_shards(): pl.pallas_call(functools.partial(sum_kernel, shards), out_shape=jax.Shape...  26.6 us
    pallas_call x1, Pallas kernels, transform_of(): pl.pallas_call(functools.partial(transform_kernel, obs_total), out_shape=...  26.2 us
    unnamed x10, local copies, waits for them, and re-layouts  3.63 us
    ppermute x1, waiting for transfers between devices, body(): lax.ppermute(packed_edge(predicted[:, :H], obs_row[:, :H]), axes, down)  2.85 us
  transfers between devices with their start and end apart: 2, of which 1 were waited for; matrix products, arithmetic and copies ran while one was open for 1% of the time, Pallas kernels for 0%

profile of v4, /device:TPU:0, one launch (start us, length us, event | category | flops | bytes accessed | tf_op | source)
XLA Modules:
  0.0 124.4 jit_solution(17088045556763447199)
XLA Ops:
  0.6 0.0 copy-start.4
  0.6 0.8 fusion.2
  1.4 1.3 %fusion.3 = (bf16[256,1024]{1,0:T(8,128)(2,1)S(1)}, bf16[256,1024]{1,0:T(8,128)(2,1)S(1)}) fusion(bf16[256,24576]{1,0:T(8,128)(2,1)} %pred_ref.1), kind=kLoop, calls=%fused_computation.20 | loop fusion | bytes 2097152 | tf_op jit(solution)/shard_map/slice | solution.py:322
  2.7 0.3 concatenate.21
  3.0 2.4 %collective-permute-start = (bf16[272,1024]{1,0:T(8,128)(2,1)S(1)}, bf16[272,1024]{1,0:T(8,128)(2,1)S(1)}, u32[]{:S(2)}, u32[]{:S(2)}) collective-permute-start(bf16[272,1024]{1,0:T(8,128)(2,1)S(1)} %concatenate.21), channel_id=1, source_target_pairs={{0,1},{1,2},{2,3},{3,4},{4,5},{5,6},{6,7},{7,8},{8,9},{9,10},{10,1... | collective-permute-start | bytes 1671176 | tf_op jit(solution)/shard_map/ppermute | solution.py:321
  5.4 0.3 concatenate.22
  5.8 1.3 %collective-permute-start.1 = (bf16[272,1024]{1,0:T(8,128)(2,1)S(1)}, bf16[272,1024]{1,0:T(8,128)(2,1)S(1)}, u32[]{:S(2)}, u32[]{:S(2)}) collective-permute-start(bf16[272,1024]{1,0:T(8,128)(2,1)S(1)} %concatenate.22), channel_id=1, source_target_pairs={{1,0},{2,1},{3,2},{4,3},{5,4},{6,5},{7,6},{8,7},{9,8},{10,9},{11,1... | collective-permute-start | bytes 1671176 | tf_op jit(solution)/shard_map/ppermute | solution.py:322
  7.7 1.1 convert_reduce_fusion
  8.9 0.0 collective-permute-done.left_ref
  8.9 2.9 %collective-permute-done.1.right_ref = bf16[272,1024]{1,0:T(8,128)(2,1)S(1)} collective-permute-done((bf16[272,1024]{1,0:T(8,128)(2,1)S(1)}, bf16[272,1024]{1,0:T(8,128)(2,1)S(1)}, u32[]{:S(2)}, u32[]{:S(2)}) %collective-permute-start.1) | collective-permute-done | bytes 557088 | tf_op jit(solution)/shard_map/ppermute | solution.py:322
  11.7 0.0 copy-start.1
  11.7 1.1 copy-done.1
  12.9 0.0 copy-start.2
  12.9 0.9 copy-done.2
  13.7 0.0 copy-start.3
  13.7 0.7 copy-done.3
  14.4 53.3 %shard_map.77 = (f32[272,256]{1,0:T(8,128)S(1)}, f32[1,24576]{1,0:T(1,128)S(1)}) custom-call(s32[8]{0:T(128)S(1)} %copy-done.3, s32[1]{0:T(128)S(6)} %copy.8.count_ref, bf16[256,24576]{1,0:T(8,128)(2,1)} %pred_ref.1, bf16[272,1024]{1,0:T(8,128)(2,1)S(1)} %collective-permute-done.left_ref, bf16[272,1024]{1,0:T(8,128)(2,1)S(1)} %collective-permute-done.1.right_ref, ...), custom_call_target="tpu_custom_call" | custom-call | tf_op jit(solution)/shard_map/pallas_call | solution.py:133
  67.7 0.7 broadcast_multiply_fusion
  68.5 0.7 select_maximum_fusion.x_ref
  69.2 26.6 %shard_map.78.x_ref = f32[16,25,128]{2,1,0:T(8,128)} custom-call(f32[16,25,128]{2,1,0:T(8,128)} %select_maximum_fusion.x_ref), custom_call_target="tpu_custom_call" | custom-call | tf_op jit(solution)/shard_map/pallas_call | solution.py:216
  95.9 0.0 copy-start
  95.9 0.9 copy-done
  96.8 26.2 %shard_map.79 = f32[256,256]{1,0:T(8,128)S(1)} custom-call(f32[16,25,128]{2,1,0:T(8,128)S(1)} %copy-done), custom_call_target="tpu_custom_call" | custom-call | tf_op jit(solution)/shard_map/pallas_call | solution.py:295
  123.0 0.0 copy-done.4
  123.0 1.4 %convolution_add_fusion = f32[512,256]{1,0:T(8,128)} fusion(f32[256,256]{1,0:T(8,128)S(1)} %shard_map.79, bf16[512,256]{1,0:T(8,128)(2,1)S(1)} %copy-done.4, f32[512]{0:T(512)S(1)} %broadcast_multiply_fusion.1), kind=kOutput, calls=%fused_computation | convolution fusion | flops 403046400 | bytes 1050624 | tf_op jit(solution)/shard_map/dot_general | solution.py:330
  (6 shorter events, 0.0 us)
Async XLA Ops:
  0.6 122.4 %copy-start.4 = (bf16[512,256]{1,0:T(8,128)(2,1)S(1)}, bf16[512,256]{1,0:T(8,128)(2,1)}, u32[]{:S(2)}) copy-start(bf16[512,256]{1,0:T(8,128)(2,1)} %param.11) | copy-start | bytes 786436
  3.0 5.8 %collective-permute-start = (bf16[272,1024]{1,0:T(8,128)(2,1)S(1)}, bf16[272,1024]{1,0:T(8,128)(2,1)S(1)}, u32[]{:S(2)}, u32[]{:S(2)}) collective-permute-start(bf16[272,1024]{1,0:T(8,128)(2,1)S(1)} %concatenate.21), channel_id=1, source_target_pairs={{0,1},{1,2},{2,3},{3,4},{4,5},{5,6},{6,7},{7,8},{8,9},{9,10},{10,1... | collective-permute-start | bytes 1671176 | tf_op jit(solution)/shard_map/ppermute | solution.py:321
  5.8 5.9 %collective-permute-start.1 = (bf16[272,1024]{1,0:T(8,128)(2,1)S(1)}, bf16[272,1024]{1,0:T(8,128)(2,1)S(1)}, u32[]{:S(2)}, u32[]{:S(2)}) collective-permute-start(bf16[272,1024]{1,0:T(8,128)(2,1)S(1)} %concatenate.22), channel_id=1, source_target_pairs={{1,0},{2,1},{3,2},{4,3},{5,4},{6,5},{7,6},{8,7},{9,8},{10,9},{11,1... | collective-permute-start | bytes 1671176 | tf_op jit(solution)/shard_map/ppermute | solution.py:322
  11.7 1.1 copy-start.1
  12.9 0.9 copy-start.2
  13.7 0.7 copy-start.3
  95.9 1.0 copy-start

commit v5 on v4

--- a/solution.py
+++ b/solution.py
@@ -172,8 +172,9 @@
     for d in range(1, shards):
         pl.semaphore_signal(barrier, inc=1, device_id=where(d)[1], device_id_type=MESH)
     pl.semaphore_wait(barrier, shards - 1)
+    order = sorted(range(1, shards), key=lambda d: -min(d, shards - d))
     first = []
-    for d in range(1, shards):
+    for d in order:
         peer, device = where(d)
         copy = pltpu.make_async_remote_copy(
             src_ref=x_ref.at[peer], dst_ref=arrived.at[d],
@@ -182,12 +183,12 @@
         copy.start()
         first.append(copy)
     total = x_ref[me]
-    for d in range(1, shards):
-        first[d - 1].wait()
+    for d in order:
+        first[order.index(d)].wait()
         total = total + arrived[d]
     chunks[...] = total
     second = []
-    for d in range(1, shards):
+    for d in order:
         peer, device = where(d)
         copy = pltpu.make_async_remote_copy(
             src_ref=chunks, dst_ref=out_ref.at[me],
@@ -196,8 +197,8 @@
         copy.start()
         second.append(copy)
     out_ref[me] = total
-    for d in range(1, shards):
-        second[d - 1].wait()
+    for d in order:
+        second[order.index(d)].wait()
 
 
 def sum_over_shards(acc, shards):

time: 125 us -> 127 us (1.016)
  Pallas kernels: 106 us -> 108 us
    pallas_call x1, Pallas kernels: 26.6 us -> 28.9 us  [sum_over_shards(): pl.pallas_call(functools.partial(sum_kernel, shards), out_shape=jax.Shape...]
where the time goes in v5:
time: 127 us
  Pallas kernels  108 us (85%)
  local copies, waits for them, and re-layouts  5.6 us (4%)
  starting transfers between devices  3.68 us (3%)
  other arithmetic  3.36 us (3%)
  waiting for transfers between devices  2.86 us (2%)
  matrix products  1.42 us (1%)
  between operations  1.42 us (1%)
    pallas_call x1, Pallas kernels, whiten_gram(): pl.pallas_call(functools.partial(whiten_kernel, tiles), grid=(tiles + 2,)...  53.3 us
    pallas_call x1, Pallas kernels, sum_over_shards(): pl.pallas_call(functools.partial(sum_kernel, shards), out_shape=jax.Shape...  28.9 us
    pallas_call x1, Pallas kernels, transform_of(): pl.pallas_call(functools.partial(transform_kernel, obs_total), out_shape=...  26.2 us
    unnamed x10, local copies, waits for them, and re-layouts  3.63 us
    ppermute x1, waiting for transfers between devices, body(): lax.ppermute(packed_edge(predicted[:, :H], obs_row[:, :H]), axes, down)  2.85 us
  transfers between devices with their start and end apart: 2, of which 1 were waited for; matrix products, arithmetic and copies ran while one was open for 1% of the time, Pallas kernels for 0%

profile of v5, /device:TPU:0, one launch (start us, length us, event | category | flops | bytes accessed | tf_op | source)
XLA Modules:
  0.0 126.7 jit_solution(6013812696930021853)
XLA Ops:
  0.6 0.0 copy-start.4
  0.6 0.8 fusion.2
  1.4 1.3 %fusion.3 = (bf16[256,1024]{1,0:T(8,128)(2,1)S(1)}, bf16[256,1024]{1,0:T(8,128)(2,1)S(1)}) fusion(bf16[256,24576]{1,0:T(8,128)(2,1)} %pred_ref.1), kind=kLoop, calls=%fused_computation.20 | loop fusion | bytes 2097152 | tf_op jit(solution)/shard_map/slice | solution.py:323
  2.7 0.3 concatenate.21
  3.0 2.4 %collective-permute-start = (bf16[272,1024]{1,0:T(8,128)(2,1)S(1)}, bf16[272,1024]{1,0:T(8,128)(2,1)S(1)}, u32[]{:S(2)}, u32[]{:S(2)}) collective-permute-start(bf16[272,1024]{1,0:T(8,128)(2,1)S(1)} %concatenate.21), channel_id=1, source_target_pairs={{0,1},{1,2},{2,3},{3,4},{4,5},{5,6},{6,7},{7,8},{8,9},{9,10},{10,1... | collective-permute-start | bytes 1671176 | tf_op jit(solution)/shard_map/ppermute | solution.py:322
  5.4 0.3 concatenate.22
  5.8 1.3 %collective-permute-start.1 = (bf16[272,1024]{1,0:T(8,128)(2,1)S(1)}, bf16[272,1024]{1,0:T(8,128)(2,1)S(1)}, u32[]{:S(2)}, u32[]{:S(2)}) collective-permute-start(bf16[272,1024]{1,0:T(8,128)(2,1)S(1)} %concatenate.22), channel_id=1, source_target_pairs={{1,0},{2,1},{3,2},{4,3},{5,4},{6,5},{7,6},{8,7},{9,8},{10,9},{11,1... | collective-permute-start | bytes 1671176 | tf_op jit(solution)/shard_map/ppermute | solution.py:323
  7.7 1.1 convert_reduce_fusion
  8.9 0.0 collective-permute-done.left_ref
  8.9 2.9 %collective-permute-done.1.right_ref = bf16[272,1024]{1,0:T(8,128)(2,1)S(1)} collective-permute-done((bf16[272,1024]{1,0:T(8,128)(2,1)S(1)}, bf16[272,1024]{1,0:T(8,128)(2,1)S(1)}, u32[]{:S(2)}, u32[]{:S(2)}) %collective-permute-start.1) | collective-permute-done | bytes 557088 | tf_op jit(solution)/shard_map/ppermute | solution.py:323
  11.7 0.0 copy-start.1
  11.7 1.1 copy-done.1
  12.9 0.0 copy-start.2
  12.9 0.9 copy-done.2
  13.7 0.0 copy-start.3
  13.7 0.7 copy-done.3
  14.4 53.3 %shard_map.77 = (f32[272,256]{1,0:T(8,128)S(1)}, f32[1,24576]{1,0:T(1,128)S(1)}) custom-call(s32[8]{0:T(128)S(1)} %copy-done.3, s32[1]{0:T(128)S(6)} %copy.8.count_ref, bf16[256,24576]{1,0:T(8,128)(2,1)} %pred_ref.1, bf16[272,1024]{1,0:T(8,128)(2,1)S(1)} %collective-permute-done.left_ref, bf16[272,1024]{1,0:T(8,128)(2,1)S(1)} %collective-permute-done.1.right_ref, ...), custom_call_target="tpu_custom_call" | custom-call | tf_op jit(solution)/shard_map/pallas_call | solution.py:133
  67.7 0.7 broadcast_multiply_fusion
  68.5 0.7 select_maximum_fusion.x_ref
  69.2 28.9 %shard_map.78.x_ref = f32[16,25,128]{2,1,0:T(8,128)} custom-call(f32[16,25,128]{2,1,0:T(8,128)} %select_maximum_fusion.x_ref), custom_call_target="tpu_custom_call" | custom-call | tf_op jit(solution)/shard_map/pallas_call | solution.py:217
  98.2 0.0 copy-start
  98.2 0.9 copy-done
  99.1 26.2 %shard_map.79 = f32[256,256]{1,0:T(8,128)S(1)} custom-call(f32[16,25,128]{2,1,0:T(8,128)S(1)} %copy-done), custom_call_target="tpu_custom_call" | custom-call | tf_op jit(solution)/shard_map/pallas_call | solution.py:296
  125.3 0.0 copy-done.4
  125.3 1.4 %convolution_add_fusion = f32[512,256]{1,0:T(8,128)} fusion(f32[256,256]{1,0:T(8,128)S(1)} %shard_map.79, bf16[512,256]{1,0:T(8,128)(2,1)S(1)} %copy-done.4, f32[512]{0:T(512)S(1)} %broadcast_multiply_fusion.1), kind=kOutput, calls=%fused_computation | convolution fusion | flops 403046400 | bytes 1050624 | tf_op jit(solution)/shard_map/dot_general | solution.py:331
  (6 shorter events, 0.0 us)
Async XLA Ops:
  0.6 124.7 %copy-start.4 = (bf16[512,256]{1,0:T(8,128)(2,1)S(1)}, bf16[512,256]{1,0:T(8,128)(2,1)}, u32[]{:S(2)}) copy-start(bf16[512,256]{1,0:T(8,128)(2,1)} %param.11) | copy-start | bytes 786436
  3.0 5.8 %collective-permute-start = (bf16[272,1024]{1,0:T(8,128)(2,1)S(1)}, bf16[272,1024]{1,0:T(8,128)(2,1)S(1)}, u32[]{:S(2)}, u32[]{:S(2)}) collective-permute-start(bf16[272,1024]{1,0:T(8,128)(2,1)S(1)} %concatenate.21), channel_id=1, source_target_pairs={{0,1},{1,2},{2,3},{3,4},{4,5},{5,6},{6,7},{7,8},{8,9},{9,10},{10,1... | collective-permute-start | bytes 1671176 | tf_op jit(solution)/shard_map/ppermute | solution.py:322
  5.8 5.9 %collective-permute-start.1 = (bf16[272,1024]{1,0:T(8,128)(2,1)S(1)}, bf16[272,1024]{1,0:T(8,128)(2,1)S(1)}, u32[]{:S(2)}, u32[]{:S(2)}) collective-permute-start(bf16[272,1024]{1,0:T(8,128)(2,1)S(1)} %concatenate.22), channel_id=1, source_target_pairs={{1,0},{2,1},{3,2},{4,3},{5,4},{6,5},{7,6},{8,7},{9,8},{10,9},{11,1... | collective-permute-start | bytes 1671176 | tf_op jit(solution)/shard_map/ppermute | solution.py:323
  11.7 1.1 copy-start.1
  12.9 0.9 copy-start.2
  13.7 0.7 copy-start.3
  98.2 1.0 copy-start
